TPU v7x, 256 devices: a whole 4x4x8 slice. The times are simulated.
256 devices in a mesh: space: 64 (over z_lo, y, x, core), chan: 4 (over z_hi).
Axes of the slice: x: 4, y: 4, z: 8 (z_hi: 4, z_lo: 2; z = z_hi * 2 + z_lo), core: 2. Of those that a mesh axis runs over, the one named last changes fastest.
Arguments:
- volume: bfloat16 [256, 128, 16, 64], P(None, 'space', 'chan'), may hold values from -6 to 6
- first_filter: bfloat16 [27, 256, 256], replicated, may hold values from -0.078125 to 0.078125
- first_bias: float32 [256], replicated, may hold values from -3 to 3
- second_filter: bfloat16 [27, 256, 256], replicated, may hold values from -0.078125 to 0.078125
- second_bias: float32 [256], replicated, may hold values from -3 to 3
Outputs:
- features: bfloat16 [256, 128, 16, 64], P('chan', 'space')
All inputs are finite; a program needn't handle non-finite values.
Results may differ from a plain program's by a relative error of at most 0.0044.
Values may be sent and summed in bfloat16 or wider, within the bound.
A program may use at most 192 MiB of HBM per device.

v0:
```python
import jax
import jax.numpy as jnp
from jax import lax
from jax.sharding import PartitionSpec as P


def padded_2(block, sides, width):
    for axis, dim in sides:
        count = lax.axis_size(axis)
        forward = [(i, i + 1) for i in range(count - 1)]
        backward = [(target, source) for source, target in forward]
        low = lax.ppermute(
            lax.slice_in_dim(block, block.shape[dim] - width, None, axis=dim), axis, forward
        )
        high = lax.ppermute(lax.slice_in_dim(block, 0, width, axis=dim), axis, backward)
        block = jnp.concatenate([low, block, high], axis=dim)
    return block


def leaky(value):
    return jnp.where(value >= 0.0, value, 0.3 * value)


def pad_sides(padded):
    return jnp.pad(padded, ((0, 0), (0, 0), (1, 1), (1, 1)))


def tap_sum(padded, filters, planes, rows_y, cols_z):
    inputs = padded.shape[0]
    outputs = filters.shape[1]
    total = jnp.zeros((outputs, planes * rows_y * cols_z), jnp.float32)
    for offset_a in range(3):
        for offset_b in range(3):
            window = jnp.concatenate(
                [
                    padded[
                        :,
                        offset_a : offset_a + planes,
                        offset_b : offset_b + rows_y,
                        offset_c : offset_c + cols_z,
                    ]
                    for offset_c in range(3)
                ],
                axis=0,
            )
            window = window.reshape(3 * inputs, planes * rows_y * cols_z)
            base = 9 * offset_a + 3 * offset_b
            stacked = jnp.concatenate([filters[base], filters[base + 1], filters[base + 2]], axis=1)
            total = total + jnp.dot(stacked, window, preferred_element_type=jnp.float32)
    return total.reshape(outputs, planes, rows_y, cols_z)


def layer(activation, filters, bias):
    slab, planes, rows_y, cols_z = activation.shape
    first_row = lax.axis_index("chan") * slab
    own_bias = lax.dynamic_slice_in_dim(bias, first_row, slab)
    own_filters = lax.dynamic_slice_in_dim(filters, first_row, slab, 1)
    whole = lax.all_gather(activation, "chan", axis=0, tiled=True)
    padded = padded_2(whole, (("space", 1),), 1)
    summed = tap_sum(pad_sides(padded), own_filters, planes, rows_y, cols_z)
    return leaky(summed + own_bias[:, None, None, None]).astype(jnp.bfloat16)


def on_device(volume, first_filter, first_bias, second_filter, second_bias):
    regrouped = lax.all_to_all(volume, "chan", split_axis=0, concat_axis=2, tiled=True)
    hidden = layer(regrouped, first_filter, first_bias)
    return layer(hidden, second_filter, second_bias)


def solution(mesh):
    in_specs = (P(None, "space", "chan", None), P(), P(), P(), P())
    out_specs = P("chan", "space", None, None)
    return jax.shard_map(
        on_device, mesh=mesh, in_specs=in_specs, out_specs=out_specs, check_vma=False
    )
```

profile of v0, /device:TPU:32, one launch (start us, length us, event | category | flops | bytes accessed | tf_op | source)
XLA Modules:
  0.0 349.1 jit_solution(13725558017042821853)
XLA Ops:
  6.5 1.3 copy.31
  8.2 18.4 %all_to_all.18 = bf16[4,2,16384]{2,1,0:T(2,128)(2,1)S(1)} all-to-all(bf16[4,2,16384]{2,1,0:T(2,128)(2,1)S(1)} %reshape.82), channel_id=1, replica_groups=mesh['space'=64,'chan'=4] {'chan'}, dimensions={0} | all-to-all | bytes 524288 | tf_op jit(solution)/shard_map/all_to_all | solution.py:65
  26.9 0.9 copy.33
  28.0 48.6 %all-gather.3.cloned.1.call-done = bf16[256,2,16,64]{3,0,2,1:T(8,128)(2,1)} async-done(((bf16[64,2,16,64]{3,0,2,1:T(8,128)(2,1)}), bf16[256,2,16,64]{3,0,2,1:T(8,128)(2,1)}) %all-gather.3.cloned.1.call-update) | async-done | bytes 1048592 | tf_op jit(solution)/shard_map/all_gather | solution.py:58
  76.5 1.7 fusion.138
  78.6 1.9 collective-permute-start
  80.5 1.1 copy.35
  81.6 8.2 %collective-permute-start.1 = (bf16[256,1,16,64]{0,3,2,1:T(8,128)(2,1)}, bf16[256,1,16,64]{0,3,2,1:T(8,128)(2,1)}, u32[]{:S(2)}, u32[]{:S(2)}) collective-permute-start(bf16[256,1,16,64]{0,3,2,1:T(8,128)(2,1)} %copy.35), channel_id=1, source_target_pairs={{4,0},{8,4},{12,8},{16,12},{20,16},{24,20},{28,24},{32,28},{36,32}... | collective-permute-start | bytes 1572872 | tf_op jit(solution)/shard_map/ppermute | solution.py:15
  89.9 1.7 dynamic-slice_bitcast_fusion.20
  91.6 1.9 dynamic-slice_bitcast_fusion.26
  93.6 1.5 copy.36
  95.1 1.5 collective-permute-done.1
  96.6 2.4 copy.37
  99.0 5.3 %select_maximum_fusion = bf16[256,4,18,66]{3,0,2,1:T(8,128)(2,1)S(1)} fusion(bf16[256,1,16,64]{3,0,2,1:T(8,128)(2,1)} %copy.37, bf16[256,2,16,64]{3,0,2,1:T(8,128)(2,1)S(1)} %copy-done, bf16[256,1,16,64]{3,0,2,1:T(8,128)(2,1)S(1)} %copy.36), kind=kLoop, calls=%fused_computation.27 | loop fusion | flops 23113728 | bytes 4530176 | tf_op jit(solution)/shard_map/concatenate | solution.py:16
  104.3 13.4 %fusion.134 = (bf16[256,2,16,64]{3,0,2,1:T(8,128)(2,1)S(1)}, bf16[256,2,16,64]{3,0,2,1:T(8,128)(2,1)S(1)}, bf16[256,2,16,64]{3,0,2,1:T(8,128)(2,1)}, bf16[256,2,...) fusion(bf16[256,4,18,66]{3,0,2,1:T(8,128)(2,1)S(1)} %select_max, ...), kind=kLoop, calls=%fused_computation.235 | loop fusion | bytes 39845888 | tf_op jit(solution)/shard_map/slice | solution.py:36
  117.7 3.2 fusion.135
  120.9 6.0 %pad_maximum_fusion.2 = (bf16[768,2,16,64]{3,0,2,1:T(8,128)(2,1)}, bf16[768,2,16,64]{3,0,2,1:T(8,128)(2,1)}) fusion(bf16[256,2,16,64]{3,0,2,1:T(8,128)(2,1)S(1)} %get-tuple-element.26, bf16[256,2,16,64]{3,0,2,1:T(8,128)(2,1)S(1)} %get-tuple-element.27, bf16[256,2,16,64]{3,0,2,1:T(8,128)(2,1)S(1)} %get-tuple-element.28, ...), kind=kLoop, calls=%fused_computation.17 | loop fusion | flops 18874368 | bytes 12582912 | tf_op jit(solution)/shard_map/concatenate | solution.py:34
  126.9 6.8 %copy.38 = bf16[768,2,16,64]{0,3,2,1:T(8,128)(2,1)} copy(bf16[768,2,16,64]{3,0,2,1:T(8,128)(2,1)} %get-tuple-element.117) | data formatting | bytes 6291456 | tf_op jit(solution)/shard_map/concatenate | solution.py:34
  133.7 13.0 %fusion.4 = (bf16[768,2,16,64]{3,0,2,1:T(8,128)(2,1)}, bf16[768,2,16,64]{3,0,2,1:T(8,128)(2,1)}, bf16[768,2,16,64]{3,0,2,1:T(8,128)(2,1)}) fusion(bf16[256,1,16,64]{3,0,2,1:T(8,128)(2,1)} %copy.37, bf16[256,2,16,64]{3,0,2,1:T(8,128)(2,1)S(1)} %copy-done, bf16[256,2,16,64]{3,0,2,1:T(8,128)(2,1)} %get-tuple-element.7, ...), kind=kLoop, calls=%fused_computation.13 | loop fusion | flops 34603008 | bytes 17825792 | tf_op jit(solution)/shard_map/concatenate | solution.py:34
  146.7 6.9 %copy.40 = bf16[768,2,16,64]{0,3,2,1:T(8,128)(2,1)} copy(bf16[768,2,16,64]{3,0,2,1:T(8,128)(2,1)} %get-tuple-element.109) | data formatting | bytes 6291456 | tf_op jit(solution)/shard_map/concatenate | solution.py:34
  153.6 9.9 %pad_maximum_fusion.3 = (bf16[768,2,16,64]{3,0,2,1:T(8,128)(2,1)}, bf16[768,2,16,64]{3,0,2,1:T(8,128)(2,1)}) fusion(bf16[256,2,16,64]{3,0,2,1:T(8,128)(2,1)} %get-tuple-element.20, bf16[256,2,16,64]{3,0,2,1:T(8,128)(2,1)} %get-tuple-element.21, bf16[256,2,16,64]{3,0,2,1:T(8,128)(2,1)} %get-tuple-element.22, bf16[256,2,16,64]{3,0,2,1:T(8,128)(2,1)S(1)} %copy-done.13, ...), kind=kLoop, calls=%fused_computation.18 | loop fusion | flops 18874368 | bytes 12582912 | tf_op jit(solution)/shard_map/concatenate | solution.py:34
  163.5 6.8 %copy.41 = bf16[768,2,16,64]{0,3,2,1:T(8,128)(2,1)} copy(bf16[768,2,16,64]{3,0,2,1:T(8,128)(2,1)} %get-tuple-element.128) | data formatting | bytes 6291456 | tf_op jit(solution)/shard_map/concatenate | solution.py:34
  170.3 6.8 %copy.42 = bf16[768,2,16,64]{0,3,2,1:T(8,128)(2,1)} copy(bf16[768,2,16,64]{3,0,2,1:T(8,128)(2,1)} %get-tuple-element.129) | data formatting | bytes 6291456 | tf_op jit(solution)/shard_map/concatenate | solution.py:34
  177.1 7.0 %copy.43 = bf16[768,2,16,64]{0,3,2,1:T(8,128)(2,1)} copy(bf16[768,2,16,64]{3,0,2,1:T(8,128)(2,1)} %get-tuple-element.108) | data formatting | bytes 6291456 | tf_op jit(solution)/shard_map/concatenate | solution.py:34
  184.1 9.9 %pad_maximum_fusion.6 = (bf16[768,2,16,64]{3,0,2,1:T(8,128)(2,1)}, bf16[768,2,16,64]{3,0,2,1:T(8,128)(2,1)}) fusion(bf16[256,2,16,64]{3,0,2,1:T(8,128)(2,1)} %get-tuple-element.12, bf16[256,2,16,64]{3,0,2,1:T(8,128)(2,1)} %get-tuple-element.13, bf16[256,2,16,64]{3,0,2,1:T(8,128)(2,1)} %get-tuple-element.14, bf16[256,2,16,64]{3,0,2,1:T(8,128)(2,1)S(1)} %copy-done.12, ...), kind=kLoop, calls=%fused_computation.21 | loop fusion | flops 18874368 | bytes 12582912 | tf_op jit(solution)/shard_map/concatenate | solution.py:34
  194.0 6.8 %copy.44 = bf16[768,2,16,64]{0,3,2,1:T(8,128)(2,1)} copy(bf16[768,2,16,64]{3,0,2,1:T(8,128)(2,1)} %get-tuple-element.130) | data formatting | bytes 6291456 | tf_op jit(solution)/shard_map/concatenate | solution.py:34
  200.8 6.8 %copy.45 = bf16[768,2,16,64]{0,3,2,1:T(8,128)(2,1)} copy(bf16[768,2,16,64]{3,0,2,1:T(8,128)(2,1)} %get-tuple-element.131) | data formatting | bytes 6291456 | tf_op jit(solution)/shard_map/concatenate | solution.py:34
  207.6 6.8 %copy.47 = bf16[768,2,16,64]{0,3,2,1:T(8,128)(2,1)} copy(bf16[768,2,16,64]{3,0,2,1:T(8,128)(2,1)} %get-tuple-element.107) | data formatting | bytes 6291456 | tf_op jit(solution)/shard_map/concatenate | solution.py:34
  214.3 7.0 %copy.48 = bf16[768,2,16,64]{0,3,2,1:T(8,128)(2,1)} copy(bf16[768,2,16,64]{3,0,2,1:T(8,128)(2,1)} %get-tuple-element.118) | data formatting | bytes 6291456 | tf_op jit(solution)/shard_map/concatenate | solution.py:34
  221.3 2.0 fusion.28
  223.4 1.1 convolution_add_fusion.14
  224.5 1.1 convolution_add_fusion.13
  226.3 1.1 convolution_add_fusion.12
  227.7 1.1 convolution_add_fusion.11
  229.4 1.1 convolution_add_fusion.10
  230.8 1.1 convolution_add_fusion.9
  232.4 1.1 convolution_add_fusion.8
  233.9 1.1 convolution_add_fusion.7
  235.4 1.0 fusion.21
  236.5 49.7 %all-gather.5.cloned.1.call-done = bf16[256,2,16,64]{3,2,1,0:T(8,128)(2,1)} async-done(((bf16[64,2,16,64]{3,2,1,0:T(8,128)(2,1)}), bf16[256,2,16,64]{3,2,1,0:T(8,128)(2,1)}) %all-gather.5.cloned.1.call-update) | async-done | bytes 1048592 | tf_op jit(solution)/shard_map/all_gather | solution.py:58
  286.2 2.8 copy.49
  289.1 1.9 collective-permute-start.2
  291.0 7.9 %collective-permute-start.3 = (bf16[256,1,16,64]{0,3,2,1:T(8,128)(2,1)S(1)}, bf16[256,1,16,64]{0,3,2,1:T(8,128)(2,1)S(1)}, u32[]{:S(2)}, u32[]{:S(2)}) collective-permute-start(bf16[256,1,16,64]{0,3,2,1:T(8,128)(2,1)S(1)} %get-tuple-element.116), channel_id=1, source_target_pairs={{4,0},{8,4},{12,8},{16,12},{20,16},{24,20},{28,24},{32,28},{36,32}... | collective-permute-start | bytes 1572872 | tf_op jit(solution)/shard_map/ppermute | solution.py:15
  298.9 1.8 dynamic-slice_bitcast_fusion.5
  300.7 3.1 collective-permute-done.2
  303.8 1.8 collective-permute-done.3
  305.5 0.8 copy-done.22
  306.3 1.1 select_maximum_fusion.2
  307.5 7.4 %fusion.136 = (bf16[256,2,16,64]{0,3,2,1:T(8,128)(2,1)S(1)}, bf16[256,2,16,64]{0,3,2,1:T(8,128)(2,1)}, bf16[256,2,16,64]{0,3,2,1:T(8,128)(2,1)}, bf16[256,2,16,6...) fusion(bf16[256,4,18,66]{0,3,2,1:T(8,128)(2,1)S(1)} %select_max, ...), kind=kLoop, calls=%fused_computation.237 | loop fusion | bytes 39845888 | tf_op jit(solution)/shard_map/slice | solution.py:36
  314.9 2.3 fusion.137
  317.5 0.9 copy-done.16
  320.4 0.9 copy-done.14
  321.9 5.6 %fusion.14 = (bf16[768,2,16,64]{0,3,2,1:T(8,128)(2,1)}, bf16[768,2,16,64]{0,3,2,1:T(8,128)(2,1)}, bf16[768,2,16,64]{0,3,2,1:T(8,128)(2,1)}) fusion(bf16[256,1,16,64]{0,3,2,1:T(8,128)(2,1)} %copy-done.22, bf16[256,2,16,64]{0,3,2,1:T(8,128)(2,1)S(1)} %copy.49, bf16[256,2,16,64]{0,3,2,1:T(8,128)(2,1)S(1)} %get-tuple-element.86, ...), kind=kLoop, calls=%fused_computation.34 | loop fusion | flops 34603008 | bytes 17825792 | tf_op jit(solution)/shard_map/concatenate | solution.py:34
  327.6 3.0 fusion.74
  330.6 1.1 fusion.110
  331.6 1.1 convolution_add_fusion.6
  332.7 1.1 convolution_add_fusion.5
  333.9 1.1 convolution_add_fusion.4
  335.7 1.1 convolution_add_fusion.3
  336.8 1.1 convolution_add_fusion.2
  337.8 1.1 convolution_add_fusion.1
  338.9 0.8 copy-done.10
  339.7 1.1 fusion.20
  341.2 1.0 fusion.22
  (127 shorter events, 8.9 us)
Async XLA Ops:
  6.5 70.0 %all-gather.3.cloned.1.call-start = ((), (), s32[]{:S(2)}) async-start(), calls=%async_computation.1 | async-start | bytes 2621440 | tf_op jit(solution)/shard_map/all_gather | solution.py:58
  27.9 61.9 %copy-start.54 = (f32[256]{0:T(256)S(1)}, f32[256]{0:T(256)}, u32[]{:S(2)}) copy-start(f32[256]{0:T(256)} %param.7) | copy-start | bytes 3076
  27.9 258.2 %all-gather.5.cloned.1.call-start = ((), (), s32[]{:S(2)}) async-start(), calls=%async_computation.2 | async-start | bytes 2621440 | tf_op jit(solution)/shard_map/all_gather | solution.py:58
  78.6 15.0 %collective-permute-start = (bf16[256,1,16,64]{0,3,2,1:T(8,128)(2,1)S(1)}, bf16[256,1,16,64]{0,3,2,1:T(8,128)(2,1)}, u32[]{:S(2)}, u32[]{:S(2)}) collective-permute-start(bf16[256,1,16,64]{0,3,2,1:T(8,128)(2,1)S(1)} %copy.34), channel_id=1, source_target_pairs={{0,4},{4,8},{8,12},{12,16},{16,20},{20,24},{24,28},{28,32},{32,36}... | collective-permute-start | bytes 1572872 | tf_op jit(solution)/shard_map/ppermute | solution.py:12
  81.6 17.4 %copy-start = (bf16[256,2,16,64]{3,0,2,1:T(8,128)(2,1)S(1)}, bf16[256,2,16,64]{3,0,2,1:T(8,128)(2,1)}, u32[]{:S(2)}) copy-start(bf16[256,2,16,64]{3,0,2,1:T(8,128)(2,1)} %all-gather.3.cloned.1.call-done) | copy-start | bytes 3145732
  81.6 15.0 %collective-permute-start.1 = (bf16[256,1,16,64]{0,3,2,1:T(8,128)(2,1)}, bf16[256,1,16,64]{0,3,2,1:T(8,128)(2,1)}, u32[]{:S(2)}, u32[]{:S(2)}) collective-permute-start(bf16[256,1,16,64]{0,3,2,1:T(8,128)(2,1)} %copy.35), channel_id=1, source_target_pairs={{4,0},{8,4},{12,8},{16,12},{20,16},{24,20},{28,24},{32,28},{36,32}... | collective-permute-start | bytes 1572872 | tf_op jit(solution)/shard_map/ppermute | solution.py:15
  146.7 6.9 %copy-start.13 = (bf16[256,2,16,64]{3,0,2,1:T(8,128)(2,1)S(1)}, bf16[256,2,16,64]{3,0,2,1:T(8,128)(2,1)}, u32[]{:S(2)}) copy-start(bf16[256,2,16,64]{3,0,2,1:T(8,128)(2,1)} %get-tuple-element.17) | copy-start | bytes 3145732
  177.1 7.0 %copy-start.12 = (bf16[256,2,16,64]{3,0,2,1:T(8,128)(2,1)S(1)}, bf16[256,2,16,64]{3,0,2,1:T(8,128)(2,1)}, u32[]{:S(2)}) copy-start(bf16[256,2,16,64]{3,0,2,1:T(8,128)(2,1)} %get-tuple-element.9) | copy-start | bytes 3145732
  214.3 7.0 %copy-start.1 = (bf16[768,2,16,64]{0,3,2,1:T(8,128)(2,1)S(1)}, bf16[768,2,16,64]{0,3,2,1:T(8,128)(2,1)}, u32[]{:S(2)}) copy-start(bf16[768,2,16,64]{0,3,2,1:T(8,128)(2,1)} %copy.38) | copy-start | bytes 9437188
  221.3 2.1 copy-start.5
  221.3 2.1 copy-start.26
  221.3 2.1 copy-start.27
  221.3 2.1 copy-start.28
  221.3 3.2 copy-start.9
  221.3 3.2 copy-start.23
  224.4 1.9 copy-start.7
  224.4 1.9 copy-start.41
  224.5 1.9 copy-start.42
  224.5 1.9 copy-start.43
  225.6 2.1 copy-start.3
  225.6 2.1 copy-start.38
  225.6 2.1 copy-start.39
  225.6 2.1 copy-start.40
  227.4 2.0 copy-start.8
  227.4 2.0 copy-start.35
  227.4 1.9 copy-start.36
  227.4 1.9 copy-start.37
  228.7 2.1 copy-start.6
  228.7 2.1 copy-start.32
  228.7 2.0 copy-start.33
  228.8 2.0 copy-start.34
  230.4 2.0 copy-start.4
  230.5 2.0 copy-start.29
  230.5 2.0 copy-start.30
  230.5 2.0 copy-start.31
  231.9 2.0 copy-start.2
  231.9 2.0 copy-start.24
  231.9 2.0 copy-start.25
  236.4 62.4 %copy-start.55 = (f32[256]{0:T(256)S(1)}, f32[256]{0:T(256)}, u32[]{:S(2)}) copy-start(f32[256]{0:T(256)} %param.9) | copy-start | bytes 3076
  289.1 14.7 %collective-permute-start.2 = (bf16[256,1,16,64]{0,3,2,1:T(8,128)(2,1)S(1)}, bf16[256,1,16,64]{0,3,2,1:T(8,128)(2,1)S(1)}, u32[]{:S(2)}, u32[]{:S(2)}) collective-permute-start(bf16[256,1,16,64]{0,3,2,1:T(8,128)(2,1)S(1)} %get-tuple-element.115), channel_id=1, source_target_pairs={{0,4},{4,8},{8,12},{12,16},{16,20},{20,24},{24,28},{28,32},{32,36}... | collective-permute-start | bytes 1572872 | tf_op jit(solution)/shard_map/ppermute | solution.py:12
  291.0 14.5 %collective-permute-start.3 = (bf16[256,1,16,64]{0,3,2,1:T(8,128)(2,1)S(1)}, bf16[256,1,16,64]{0,3,2,1:T(8,128)(2,1)S(1)}, u32[]{:S(2)}, u32[]{:S(2)}) collective-permute-start(bf16[256,1,16,64]{0,3,2,1:T(8,128)(2,1)S(1)} %get-tuple-element.116), channel_id=1, source_target_pairs={{4,0},{8,4},{12,8},{16,12},{20,16},{24,20},{28,24},{32,28},{36,32}... | collective-permute-start | bytes 1572872 | tf_op jit(solution)/shard_map/ppermute | solution.py:15
  305.5 0.8 copy-start.22
  314.9 2.3 copy-start.19
  314.9 2.3 copy-start.20
  314.9 2.3 copy-start.21
  317.2 1.2 copy-start.16
  317.2 1.5 copy-start.17
  317.2 1.8 copy-start.18
  320.1 1.2 copy-start.14
  320.1 1.5 copy-start.15
  327.5 3.0 copy-start.52
  327.5 3.0 copy-start.53
  327.6 4.1 %copy-start.51 = (bf16[64,256]{1,0:T(8,128)(2,1)S(1)}, bf16[64,256]{1,0:T(8,128)(2,1)}, u32[]{:S(2)}) copy-start(bf16[64,256]{1,0:T(8,128)(2,1)} %get-tuple-element.46) | copy-start | bytes 98308
  332.7 1.1 copy-start.48
  332.7 1.1 copy-start.49
  332.7 1.1 copy-start.50
  333.8 1.9 copy-start.11
  333.8 1.9 copy-start.45
  333.8 1.9 copy-start.46
  333.8 1.9 copy-start.47
  334.9 1.8 copy-start.44
  337.8 1.9 copy-start.10
Sparse Core Ops, SparseCore 0:
  28.0 48.4 all-gather.2
  236.6 49.5 all-gather.4
where the time goes:
time: 353 us; the launch traced here: 349 us
  local copies, waits for them, and re-layouts  115 us (33%)
  waiting for transfers between devices  105 us (30%)
  other arithmetic  54.9 us (16%)
  matrix products  22 us (6%)
  starting transfers between devices  19.9 us (6%)
  blocking collectives  18.4 us (5%)
  between operations  14.1 us (4%)
    all_gather x2, waiting for transfers between devices, layer(): whole = lax.all_gather(activation, 'chan', axis=0, tiled=True)  98.3 us
    concatenate x9, local copies, waits for them, and re-layouts, tap_sum(): jnp.concatenate([padded[:, offset_a:offset_a + planes, offset_b:offset_b...  61.6 us
    concatenate x11, other arithmetic, tap_sum(): jnp.concatenate([padded[:, offset_a:offset_a + planes, offset_b:offset_b...  46.4 us
    slice x4, local copies, waits for them, and re-layouts, tap_sum(): padded[:, offset_a:offset_a + planes, offset_b:offset_b + rows_y, offset_...  26.3 us
    dot_general x18, matrix products, tap_sum(): total = total + jnp.dot(stacked, window, preferred_element_type=jnp.float32)  22 us
    all_to_all x1, blocking collectives, on_device(): lax.all_to_all(volume, 'chan', split_axis=0, concat_axis=2, tiled=True)  18.4 us
    ppermute x2, starting transfers between devices, padded_2(): lax.ppermute(lax.slice_in_dim(block, 0, width, axis=dim), axis, backward)  16 us
    unnamed x115, local copies, waits for them, and re-layouts  10 us
  transfers between devices with their start and end apart: 6, of which 5 were waited for; matrix products, arithmetic and copies ran while one was open for 2% of the time, Pallas kernels for 0%

commit v1 on v0

v1 whole, which is shorter than its diff:
```python
import jax
import jax.numpy as jnp
from jax import lax
from jax.experimental import pallas as pl
from jax.experimental.pallas import tpu as pltpu
from jax.sharding import PartitionSpec as P

MESH = pl.DeviceIdType.MESH
F32, BF16 = jnp.float32, jnp.bfloat16
CHAN = 4
SLAB = 64


def leaky(value):
    return jnp.where(value >= 0.0, value, 0.3 * value)


def nt(a, b):
    return lax.dot_general(a, b, (((1,), (1,)), ((), ())), preferred_element_type=F32)


def window(padded, a, b, inner):
    if inner:
        return padded[a : a + 2, 1 + b : 3 + b].reshape(256, 256)
    rows = [padded[a + p, 3 * r + b] for p in range(2) for r in range(2)]
    return jnp.concatenate(rows, axis=0)


def shifted_rows(low, mid, high):
    rows = low.shape[0]
    z = lax.broadcasted_iota(jnp.int32, low.shape, 0) % 64
    up = jnp.where(z == 0, 0.0, pltpu.roll(low, 1, 0))
    down = jnp.where(z == 63, 0.0, pltpu.roll(high, rows - 1, 0))
    return mid + up + down


def shifted_lanes(low, mid, high):
    parts = []
    for first in range(0, low.shape[1], 128):
        cut = slice(first, first + 128)
        z = lax.broadcasted_iota(jnp.int32, (low.shape[0], 128), 1) % 64
        up = jnp.where(z == 0, 0.0, pltpu.roll(low[:, cut], 1, 1))
        down = jnp.where(z == 63, 0.0, pltpu.roll(high[:, cut], 127, 1))
        parts.append(mid[:, cut] + up + down)
    return jnp.concatenate(parts, axis=1)


def accumulate(padded, filters, inner, channels_first):
    sums = [None] * 3
    for a in range(3):
        for b in range(3):
            voxels = window(padded, a, b, inner)
            for c in range(3):
                taps = filters[9 * a + 3 * b + c]
                term = nt(taps, voxels) if channels_first else nt(voxels, taps)
                sums[c] = term if sums[c] is None else sums[c] + term
    return sums


def kernel(
    vol, f1, b1, f2, b2, out,
    one, two, w1, w2, mine, got, rows, local, xs, xr, ys, yr, cs, cr, ts, tr,
):
    s, j = lax.axis_index("space"), lax.axis_index("chan")
    last = lax.axis_size("space") - 1
    has_lo, has_hi = s > 0, s < last
    has_up, has_down = j > 0, j < CHAN - 1

    load_vol = pltpu.make_async_copy(vol, one.at[1:3, 1:5], local.at[0])
    load_f1 = pltpu.make_async_copy(f1, w1, local.at[1])
    load_f2 = pltpu.make_async_copy(f2, w2, local.at[2])
    load_vol.start()
    load_f1.start()
    load_f2.start()

    for block in (one, two):
        for absent, place in (
            (s == 0, (0,)),
            (s == last, (3,)),
            (j == 0, (slice(None), 0)),
            (j == CHAN - 1, (slice(None), 5)),
        ):
            @pl.when(absent)
            def _(block=block, place=place):
                block[place] = jnp.zeros(block.at[place].shape, BF16)

    barrier = pltpu.get_barrier_semaphore()
    for step in range(1, CHAN):
        pl.semaphore_signal(barrier, inc=1, device_id=(s, (j + step) % CHAN), device_id_type=MESH)
    for there, who in ((has_lo, s - 1), (has_hi, s + 1)):
        @pl.when(there)
        def _(who=who):
            pl.semaphore_signal(barrier, inc=1, device_id=(who, j), device_id_type=MESH)
    pl.semaphore_wait(barrier, CHAN - 1 + has_lo.astype(jnp.int32) + has_hi.astype(jnp.int32))

    def remote(src, dst, send, recv, to):
        return pltpu.make_async_remote_copy(
            src_ref=src, dst_ref=dst, send_sem=send, recv_sem=recv, device_id=to, device_id_type=MESH
        )

    def x_copies(n, block, low_src, high_src):
        return (
            (has_lo, has_hi, remote(low_src, block.at[3, 1:5], xs.at[n, 0], xr.at[n, 0], (s - 1, j))),
            (has_hi, has_lo, remote(high_src, block.at[0, 1:5], xs.at[n, 1], xr.at[n, 1], (s + 1, j))),
        )

    def y_copies(n, block, up_src, down_src):
        return (
            (has_up, has_down, remote(up_src, block.at[1:3, 5], ys.at[n, 0], yr.at[n, 0], (s, j - 1))),
            (has_down, has_up, remote(down_src, block.at[1:3, 0], ys.at[n, 1], yr.at[n, 1], (s, j + 1))),
        )

    def corner_copies(n, block):
        copies = []
        for r, (row, there) in enumerate(((0, has_up), (5, has_down))):
            copies.append((
                has_lo & there, has_hi & there,
                remote(block.at[1, row], block.at[3, row], cs.at[n, r, 0], cr.at[n, r, 0], (s - 1, j)),
            ))
            copies.append((
                has_hi & there, has_lo & there,
                remote(block.at[2, row], block.at[0, row], cs.at[n, r, 1], cr.at[n, r, 1], (s + 1, j)),
            ))
        return copies

    def start(copies):
        for sends, _, copy in copies:
            pl.when(sends)(copy.start)

    def arrived(copies):
        for _, receives, copy in copies:
            pl.when(receives)(copy.wait_recv)

    def left(copies):
        for sends, _, copy in copies:
            pl.when(sends)(copy.wait_send)

    y1 = y_copies(0, one, vol.at[:, 0], vol.at[:, 3])
    x1 = x_copies(0, one, vol.at[0], vol.at[1])
    c1 = corner_copies(0, one)
    start(y1)
    start(x1)
    load_vol.wait()
    load_f1.wait()
    arrived(y1)
    start(c1)
    arrived(x1)

    bias1 = b1[...]
    inner = leaky(shifted_rows(*accumulate(one, w1, True, False)) + bias1).astype(BF16)
    two[1:3, 2:4] = inner.reshape(2, 2, 64, 256)
    arrived(c1)
    outer = leaky(shifted_rows(*accumulate(one, w1, False, False)) + bias1).astype(BF16)
    outer = outer.reshape(2, 2, 64, 256)
    two[1:3, 1] = outer[:, 0]
    two[1:3, 4] = outer[:, 1]

    y2 = y_copies(1, two, two.at[1:3, 1], two.at[1:3, 4])
    x2 = x_copies(1, two, two.at[1, 1:5], two.at[2, 1:5])
    c2 = corner_copies(1, two)
    start(y2)
    start(x2)
    load_f2.wait()
    bias2 = jnp.transpose(jnp.broadcast_to(b2[...], (8, 256)))[:, :1]

    def turn(n):
        copies = []
        for step in (2, 1, 3):
            to = (j + step) % CHAN
            copies.append(remote(
                mine.at[n, pl.ds(pl.multiple_of(to * SLAB, SLAB), SLAB)], got.at[n, j],
                ts.at[n, step - 1], tr.at[n, step - 1], (s, to),
            ))
        return copies

    arrived(x2)
    arrived(y2)
    start(c2)
    sent = [turn(0), turn(1)]
    for n in range(2):
        if n == 1:
            arrived(c2)
        block = leaky(shifted_lanes(*accumulate(two, w2, n == 0, True)) + bias2).astype(BF16)
        mine[n] = block
        for copy in sent[n]:
            copy.start()
        got[n, j] = mine[n, pl.ds(pl.multiple_of(j * SLAB, SLAB), SLAB)]
    for copy in sent[0] + sent[1]:
        copy.wait_recv()

    for n in range(2):
        for source in range(CHAN):
            slab = got[n, source].astype(F32)
            low, high = (1, 2) if n == 0 else (0, 3)
            for p in range(2):
                pair = slab[:, 128 * p : 128 * p + 128]
                rows[p, pl.ds((4 * source + low) * SLAB, SLAB)] = pair
                rows[p, pl.ds((4 * source + high) * SLAB, SLAB)] = pltpu.roll(pair, 64, 1)
    for o in range(SLAB):
        for p in range(2):
            out[o, p] = rows[p, pl.ds(o, 16, stride=SLAB), :][:, :64].astype(BF16)

    left(y1)
    left(x1)
    left(c1)
    left(y2)
    left(x2)
    left(c2)
    for copy in sent[0] + sent[1]:
        copy.wait_send()


def on_device(volume, first_filter, first_bias, second_filter, second_bias):
    voxels = jnp.transpose(volume, (1, 2, 3, 0))
    hbm, vmem = pl.BlockSpec(memory_space=pltpu.HBM), pl.BlockSpec(memory_space=pltpu.VMEM)
    dma = pltpu.SemaphoreType.DMA
    return pl.pallas_call(
        kernel,
        out_shape=jax.ShapeDtypeStruct((64, 2, 16, 64), BF16),
        in_specs=[hbm, hbm, vmem, hbm, vmem],
        out_specs=vmem,
        scratch_shapes=[
            pltpu.VMEM((4, 6, 64, 256), BF16),
            pltpu.VMEM((4, 6, 64, 256), BF16),
            pltpu.VMEM((27, 256, 256), BF16),
            pltpu.VMEM((27, 256, 256), BF16),
            pltpu.VMEM((2, 256, 256), BF16),
            pltpu.VMEM((2, CHAN, SLAB, 256), BF16),
            pltpu.VMEM((2, 16 * SLAB, 128), F32),
            dma((3,)),
            dma((2, 2)),
            dma((2, 2)),
            dma((2, 2)),
            dma((2, 2)),
            dma((2, 2, 2)),
            dma((2, 2, 2)),
            dma((2, 3)),
            dma((2, 3)),
        ],
        compiler_params=pltpu.CompilerParams(
            collective_id=0, has_side_effects=True, vmem_limit_bytes=40 * 2**20
        ),
        cost_estimate=pl.CostEstimate(flops=3_623_878_656, bytes_accessed=8_000_000, transcendentals=0),
    )(voxels, first_filter, first_bias.reshape(1, 256), second_filter, second_bias.reshape(1, 256))


def solution(mesh):
    in_specs = (P(None, "space", "chan", None), P(), P(), P(), P())
    out_specs = P("chan", "space", None, None)
    return jax.shard_map(
        on_device, mesh=mesh, in_specs=in_specs, out_specs=out_specs, check_vma=False
    )
```

time: 353 us -> 48.8 us (0.14); the launches traced: 349 us -> 48.6 us
  local copies, waits for them, and re-layouts: 115 us -> 7.1 us
  waiting for transfers between devices: 105 us -> 0 us
  other arithmetic: 54.9 us -> 0 us
  Pallas kernels: 0 us -> 41.5 us
  matrix products: 22 us -> 0 us
  starting transfers between devices: 19.9 us -> 0 us
  blocking collectives: 18.4 us -> 0 us
  between operations: 14.1 us -> 0.01 us
    all_gather x2 -> x0, waiting for transfers between devices: 98.3 us -> none  [layer(): whole = lax.all_gather(activation, 'chan', axis=0, tiled=True)]
    concatenate x9 -> x0, local copies, waits for them, and re-layouts: 61.6 us -> none  [tap_sum(): jnp.concatenate([padded[:, offset_a:offset_a + planes, offset_b:offset_b...]
    concatenate x13 -> x0, other arithmetic: 52.8 us -> none  [the longest x11 46.4 us: tap_sum(): jnp.concatenate([padded[:, offset_a:offset_a + planes, offset_b:offset_b...]
    pallas_call x0 -> x1, Pallas kernels: none -> 41.5 us  [on_device(): pl.pallas_call(kernel, out_shape=jax.ShapeDtypeStruct((64, 2, 16, 64), BF...]
    slice x8 -> x0, local copies, waits for them, and re-layouts: 29.5 us -> none  [the longest x4 26.3 us: tap_sum(): padded[:, offset_a:offset_a + planes, offset_b:offset_b + rows_y, offset_...]
    dot_general x18 -> x0, matrix products: 22 us -> none  [tap_sum(): total = total + jnp.dot(stacked, window, preferred_element_type=jnp.float32)]
    ppermute x4 -> x0, starting transfers between devices: 19.9 us -> none  [the longest x2 16 us: padded_2(): lax.ppermute(lax.slice_in_dim(block, 0, width, axis=dim), axis, backward)]
    all_to_all x1 -> x0, blocking collectives: 18.4 us -> none  [on_device(): lax.all_to_all(volume, 'chan', split_axis=0, concat_axis=2, tiled=True)]
  transfers between devices with their start and end apart: 6 -> 0, of which waited for: 5 -> 0; matrix products, arithmetic and copies ran while one was open for 2% -> 0% of each run, Pallas kernels for 0% -> 0%
where the time goes in v1:
time: 48.8 us; the launch traced here: 48.6 us
  Pallas kernels  41.5 us (85%)
  local copies, waits for them, and re-layouts  7.1 us (15%)
    pallas_call x1, Pallas kernels, on_device(): pl.pallas_call(kernel, out_shape=jax.ShapeDtypeStruct((64, 2, 16, 64), BF...  41.5 us
    unnamed x11, local copies, waits for them, and re-layouts  7.1 us

profile of v1, /device:TPU:32, one launch (start us, length us, event | category | flops | bytes accessed | tf_op | source)
XLA Modules:
  0.0 48.6 jit_solution(12945449721688262304)
XLA Ops:
  0.0 0.0 copy-start
  0.0 2.0 %copy-done = bf16[27,256,256]{2,1,0:T(8,128)(2,1)S(1)} copy-done((bf16[27,256,256]{2,1,0:T(8,128)(2,1)S(1)}, bf16[27,256,256]{2,1,0:T(8,128)(2,1)}, u32[]{:S(2)}) %copy-start) | copy-done | bytes 3538968
  2.0 0.0 copy-start.1
  2.0 2.0 %copy-done.1 = bf16[27,256,256]{2,1,0:T(8,128)(2,1)S(1)} copy-done((bf16[27,256,256]{2,1,0:T(8,128)(2,1)S(1)}, bf16[27,256,256]{2,1,0:T(8,128)(2,1)}, u32[]{:S(2)}) %copy-start.1) | copy-done | bytes 3538968
  4.0 0.0 copy-start.2
  4.0 0.9 %copy-done.2 = bf16[256,2,4,64]{0,3,2,1:T(8,128)(2,1)S(1)} copy-done((bf16[256,2,4,64]{0,3,2,1:T(8,128)(2,1)S(1)}, bf16[256,2,4,64]{0,3,2,1:T(8,128)(2,1)}, u32[]{:S(2)}) %copy-start.2) | copy-done | bytes 262168
  5.0 0.0 copy-start.3
  5.0 0.7 %copy-done.3 = f32[256]{0:T(256)S(1)} copy-done((f32[256]{0:T(256)S(1)}, f32[256]{0:T(256)}, u32[]{:S(2)}) %copy-start.3) | copy-done | bytes 1048
  5.6 0.0 copy-start.4
  5.6 0.7 %copy-done.4 = f32[256]{0:T(256)S(1)} copy-done((f32[256]{0:T(256)S(1)}, f32[256]{0:T(256)}, u32[]{:S(2)}) %copy-start.4) | copy-done | bytes 1048
  6.3 41.5 %shard_map.55 = bf16[64,2,16,64]{3,2,1,0:T(8,128)(2,1)S(1)} custom-call(bf16[2,4,64,256]{3,2,1,0:T(8,128)(2,1)S(1)} %bitcast.3, bf16[27,256,256]{2,1,0:T(8,128)(2,1)S(1)} %copy-done, f32[1,256]{1,0:T(1,128)S(1)} %bitcast.4, bf16[27,256,256]{2,1,0:T(8,128)(2,1)S(1)} %copy-done.1, f32[1,256]{1,0:T(1,128)S(1)} %bitcast.5), custom_call_target="tpu_custom_call" | custom-call | flops 3623878656 | bytes 8000000 | tf_op jit(solution)/shard_map/pallas_call | solution.py:217
  47.8 0.8 %copy.7 = bf16[64,2,16,64]{3,2,1,0:T(8,128)(2,1)} copy(bf16[64,2,16,64]{3,2,1,0:T(8,128)(2,1)S(1)} %shard_map.55) | data formatting | bytes 524288
Async XLA Ops:
  0.0 2.0 %copy-start = (bf16[27,256,256]{2,1,0:T(8,128)(2,1)S(1)}, bf16[27,256,256]{2,1,0:T(8,128)(2,1)}, u32[]{:S(2)}) copy-start(bf16[27,256,256]{2,1,0:T(8,128)(2,1)} %f1.1) | copy-start | bytes 10616836
  2.0 2.0 %copy-start.1 = (bf16[27,256,256]{2,1,0:T(8,128)(2,1)S(1)}, bf16[27,256,256]{2,1,0:T(8,128)(2,1)}, u32[]{:S(2)}) copy-start(bf16[27,256,256]{2,1,0:T(8,128)(2,1)} %f2.1) | copy-start | bytes 10616836
  4.0 0.9 %copy-start.2 = (bf16[256,2,4,64]{0,3,2,1:T(8,128)(2,1)S(1)}, bf16[256,2,4,64]{0,3,2,1:T(8,128)(2,1)}, u32[]{:S(2)}) copy-start(bf16[256,2,4,64]{0,3,2,1:T(8,128)(2,1)} %param.5) | copy-start | bytes 786436
  5.0 0.7 %copy-start.3 = (f32[256]{0:T(256)S(1)}, f32[256]{0:T(256)}, u32[]{:S(2)}) copy-start(f32[256]{0:T(256)} %param.7) | copy-start | bytes 3076
  5.6 0.7 %copy-start.4 = (f32[256]{0:T(256)S(1)}, f32[256]{0:T(256)}, u32[]{:S(2)}) copy-start(f32[256]{0:T(256)} %param.9) | copy-start | bytes 3076

commit v2 on v0

v2 whole, which is shorter than its diff:
```python
import jax
import jax.numpy as jnp
from jax import lax
from jax.experimental import pallas as pl
from jax.experimental.pallas import tpu as pltpu
from jax.sharding import PartitionSpec as P

MESH = pl.DeviceIdType.MESH
F32, BF16 = jnp.float32, jnp.bfloat16
CHAN = 4
SLAB = 64
E2, E1, O0, O1, I1 = range(-2, 3)
PLANE_ONE = {E1: 0, E2: 1, O0: 2, O1: 3, I1: 4}
ROW_ONE = {0: 0, 1: 1, 2: 2, 3: 3, -1: 4, 4: 5, -2: 6, 5: 7}
PLANE_TWO = {E1: 0, O0: 1, O1: 2, I1: 3}
ROW_TWO = {0: 0, 1: 1, 2: 2, 3: 3, -1: 4, 4: 5}


def leaky(value):
    return jnp.where(value >= 0.0, value, 0.3 * value)


def nt(a, b):
    return lax.dot_general(a, b, (((1,), (1,)), ((), ())), preferred_element_type=F32)


def shifted_rows(low, mid, high):
    rows = low.shape[0]
    z = lax.broadcasted_iota(jnp.int32, low.shape, 0) % 64
    up = jnp.where(z == 0, 0.0, pltpu.roll(low, 1, 0))
    down = jnp.where(z == 63, 0.0, pltpu.roll(high, rows - 1, 0))
    return mid + up + down


def shifted_lanes(low, mid, high):
    parts = []
    for first in range(0, low.shape[1], 128):
        cut = slice(first, first + 128)
        z = lax.broadcasted_iota(jnp.int32, (low.shape[0], 128), 1) % 64
        up = jnp.where(z == 0, 0.0, pltpu.roll(low[:, cut], 1, 1))
        down = jnp.where(z == 63, 0.0, pltpu.roll(high[:, cut], 127, 1))
        parts.append(mid[:, cut] + up + down)
    return jnp.concatenate(parts, axis=1)


def accumulate(block, plane_of, row_of, planes, rows, filters, channels_first):
    sums = [None] * 3
    for a in range(3):
        for b in range(3):
            pieces = [block[plane_of[p + a - 1], row_of[y + b - 1]] for p in planes for y in rows]
            voxels = jnp.concatenate(pieces, axis=0)
            for c in range(3):
                taps = filters[9 * a + 3 * b + c]
                term = nt(taps, voxels) if channels_first else nt(voxels, taps)
                sums[c] = term if sums[c] is None else sums[c] + term
    return sums


def kernel(
    vol, f1, b1, f2, b2, out,
    one, two, w1, w2, bias, mine, got, rows, local, send_sems, recv_sems, relay,
):
    s, j = lax.axis_index("space"), lax.axis_index("chan")
    flip = s % 2
    sib, ext = s + 1 - 2 * flip, s - 1 + 2 * flip
    has_ext = (ext >= 0) & (ext < lax.axis_size("space"))
    has_up, has_down = j > 0, j < CHAN - 1
    here = (s, j)

    loads = [
        pltpu.make_async_copy(vol.at[flip], one.at[2, 0:4], local.at[0]),
        pltpu.make_async_copy(vol.at[1 - flip], one.at[3, 0:4], local.at[1]),
    ]
    for n, (src, dst) in enumerate(((f1, w1), (f2, w2))):
        for a in range(3):
            first = 9 * (a + flip * (2 - 2 * a))
            loads.append(pltpu.make_async_copy(src.at[pl.ds(first, 9)], dst.at[9 * a : 9 * a + 9], local.at[2 + 3 * n + a]))
    loads.append(pltpu.make_async_copy(b1, bias.at[0], local.at[8]))
    loads.append(pltpu.make_async_copy(b2, bias.at[1], local.at[9]))
    for load in loads[:2]:
        load.start()

    barrier = pltpu.get_barrier_semaphore()
    pl.semaphore_signal(barrier, inc=1, device_id=(sib, j), device_id_type=MESH)
    for there, who in ((has_ext, (ext, j)), (has_up, (s, j - 1)), (has_down, (s, j + 1))):
        @pl.when(there)
        def _(who=who):
            pl.semaphore_signal(barrier, inc=1, device_id=who, device_id_type=MESH)
    for load in loads[2:]:
        load.start()

    def clear(ref, place):
        ref[place] = jnp.zeros(ref.at[place].shape, BF16)

    for block, outer, above, below in ((one, slice(0, 2), (4, 6), (5, 7)), (two, 0, (4,), (5,))):
        pl.when(~has_ext)(lambda block=block, outer=outer: clear(block, (outer,)))
        for there, places in ((has_up, above), (has_down, below)):
            for place in places:
                pl.when(~there)(lambda block=block, place=place: clear(block, (slice(None), place)))

    used = []

    def remote(src, dst, to, sends, receives):
        n = len(used)
        copy = pltpu.make_async_remote_copy(
            src_ref=src, dst_ref=dst, send_sem=send_sems.at[n], recv_sem=recv_sems.at[n],
            device_id=to, device_id_type=MESH,
        )
        used.append((copy, sends, receives))
        return used[-1]

    def start(*copies):
        for copy, sends, _ in copies:
            copy.start() if sends is True else pl.when(sends)(copy.start)

    def arrived(*copies):
        for copy, _, receives in copies:
            copy.wait_recv() if receives is True else pl.when(receives)(copy.wait_recv)

    sibling, outside, above, below = (sib, j), (ext, j), (s, j - 1), (s, j + 1)
    own = slice(0, 4)
    to_sib = remote(one.at[3, own], one.at[4, own], sibling, True, True)
    to_ext = remote(one.at[2:4, own], one.at[0:2, own], outside, has_ext, has_ext)
    near = (
        remote(one.at[2:4, 0], one.at[2:4, ROW_ONE[4]], above, has_up, has_down),
        remote(one.at[2:4, 3], one.at[2:4, ROW_ONE[-1]], below, has_down, has_up),
    )
    far = (
        remote(one.at[2:4, 1], one.at[2:4, ROW_ONE[5]], above, has_up, has_down),
        remote(one.at[2:4, 2], one.at[2:4, ROW_ONE[-2]], below, has_down, has_up),
    )

    def corners(y_up, y_down):
        copies = []
        for y, there in ((y_up, has_up), (y_down, has_down)):
            r = ROW_ONE[y]
            copies.append(remote(one.at[2:4, r], one.at[0:2, r], outside, has_ext & there, has_ext & there))
            copies.append(remote(one.at[3, r], one.at[4, r], sibling, there, there))
        return copies

    near_corners, far_corners = corners(-1, 4), corners(-2, 5)
    inner_two = remote(two.at[2, own], two.at[3, own], sibling, True, True)
    outer_two = remote(two.at[2, 4:6], two.at[3, 4:6], sibling, True, True)
    turns = []
    for n in range(2):
        turns.append([])
        for step in (2, 1, 3):
            to = (j + step) % CHAN
            turns[n].append(remote(
                mine.at[n, pl.ds(pl.multiple_of(to * SLAB, SLAB), SLAB)], got.at[n, j], (s, to), True, True
            ))

    loads[0].wait()
    loads[1].wait()
    pl.semaphore_wait(
        barrier, 1 + has_ext.astype(jnp.int32) + has_up.astype(jnp.int32) + has_down.astype(jnp.int32)
    )
    start(*near, to_ext, to_sib, *far)

    def hidden(y_pair):
        sums = accumulate(one, PLANE_ONE, ROW_ONE, (E1, O0, O1), y_pair, w1, False)
        value = leaky(shifted_rows(*sums) + bias[0]).astype(BF16).reshape(3, 2, 64, 256)
        for i, y in enumerate(y_pair):
            two[0:3, ROW_TWO[y]] = value[:, i]
        pl.when(~has_ext)(lambda: [clear(two, (0, ROW_TWO[y])) for y in y_pair] and None)

    def features(n, y_pair):
        sums = accumulate(two, PLANE_TWO, ROW_TWO, (O0, O1), y_pair, w2, True)
        mine[n] = leaky(shifted_lanes(*sums) + bias2).astype(BF16)
        start(*turns[n])
        got[n, j] = mine[n, pl.ds(pl.multiple_of(j * SLAB, SLAB), SLAB)]

    def regroup(n, y_pair):
        for source in range(CHAN):
            slab = got[n, source].astype(F32)
            for q in range(2):
                pair = slab[:, 128 * q : 128 * q + 128]
                p = q + flip * (1 - 2 * q)
                rows[p, pl.ds((4 * source + y_pair[0]) * SLAB, SLAB)] = pair
                rows[p, pl.ds((4 * source + y_pair[1]) * SLAB, SLAB)] = pltpu.roll(pair, 64, 1)

    arrived(*near)
    start(*near_corners)
    for at, tell in ((1, 0), (2, 3)):
        @pl.when(j == at)
        def _(tell=tell):
            pl.semaphore_signal(relay, inc=1, device_id=(s, tell), device_id_type=MESH)
    for load in loads[2:5] + loads[8:]:
        load.wait()
    arrived(to_ext, to_sib)
    hidden((1, 2))
    arrived(*far)
    start(*far_corners)
    arrived(*near_corners)
    hidden((0, 3))
    start(inner_two)
    arrived(*far_corners)
    hidden((-1, 4))
    for there, r in ((has_up, 4), (has_down, 5)):
        pl.when(~there)(lambda r=r: clear(two, (slice(0, 3), r)))
    start(outer_two)
    for load in loads[5:8]:
        load.wait()
    bias2 = jnp.transpose(jnp.broadcast_to(bias[1], (8, 256)))[:, :1]
    arrived(inner_two)
    pl.when((j == 0) | (j == CHAN - 1))(lambda: pl.semaphore_wait(relay, 1))
    features(0, (1, 2))
    arrived(outer_two)
    features(1, (0, 3))
    arrived(*turns[0])
    regroup(0, (1, 2))
    arrived(*turns[1])
    regroup(1, (0, 3))
    for o in range(SLAB):
        for p in range(2):
            out[o, p] = rows[p, pl.ds(o, 16, stride=SLAB), :][:, :64].astype(BF16)

    for copy, sends, _ in used:
        copy.wait_send() if sends is True else pl.when(sends)(copy.wait_send)


def on_device(volume, first_filter, first_bias, second_filter, second_bias):
    voxels = jnp.transpose(volume, (1, 2, 3, 0))
    hbm, vmem = pl.BlockSpec(memory_space=pltpu.HBM), pl.BlockSpec(memory_space=pltpu.VMEM)
    dma = pltpu.SemaphoreType.DMA
    return pl.pallas_call(
        kernel,
        out_shape=jax.ShapeDtypeStruct((64, 2, 16, 64), BF16),
        in_specs=[hbm] * 5,
        out_specs=vmem,
        scratch_shapes=[
            pltpu.VMEM((5, 8, 64, 256), BF16),
            pltpu.VMEM((4, 6, 64, 256), BF16),
            pltpu.VMEM((27, 256, 256), BF16),
            pltpu.VMEM((27, 256, 256), BF16),
            pltpu.VMEM((2, 1, 256), F32),
            pltpu.VMEM((2, 256, 256), BF16),
            pltpu.VMEM((2, CHAN, SLAB, 256), BF16),
            pltpu.VMEM((2, 16 * SLAB, 128), F32),
            dma((10,)),
            dma((22,)),
            dma((22,)),
            pltpu.SemaphoreType.REGULAR,
        ],
        compiler_params=pltpu.CompilerParams(
            collective_id=0, has_side_effects=True, vmem_limit_bytes=62 * 2**20
        ),
        cost_estimate=pl.CostEstimate(flops=5_900_000_000, bytes_accessed=8_000_000, transcendentals=0),
    )(voxels, first_filter, first_bias.reshape(1, 256), second_filter, second_bias.reshape(1, 256))


def solution(mesh):
    in_specs = (P(None, "space", "chan", None), P(), P(), P(), P())
    out_specs = P("chan", "space", None, None)
    return jax.shard_map(
        on_device, mesh=mesh, in_specs=in_specs, out_specs=out_specs, check_vma=False
    )
```

time: 353 us -> 41.2 us (0.12)
  the two profiles are of different devices: /device:TPU:32 before, /device:TPU:31 now
where the time goes in v2:
time: 41.2 us; the launch traced here: 41.1 us
  Pallas kernels  39.2 us (95%)
  local copies, waits for them, and re-layouts  1.87 us (5%)
    pallas_call x1, Pallas kernels, on_device(): pl.pallas_call(kernel, out_shape=jax.ShapeDtypeStruct((64, 2, 16, 64), BF...  39.2 us
    unnamed x1, local copies, waits for them, and re-layouts  1.87 us

profile of v2, /device:TPU:31, one launch (start us, length us, event | category | flops | bytes accessed | tf_op | source)
XLA Modules:
  0.0 41.1 jit_solution(11223300045170847621)
XLA Ops:
  0.0 39.2 %shard_map.55 = bf16[64,2,16,64]{3,2,1,0:T(8,128)(2,1)} custom-call(bf16[2,4,64,256]{3,2,1,0:T(8,128)(2,1)} %bitcast.3, bf16[27,256,256]{2,1,0:T(8,128)(2,1)} %f1.1, f32[1,256]{1,0:T(1,128)} %bitcast.4, bf16[27,256,256]{2,1,0:T(8,128)(2,1)} %f2.1, f32[1,256]{1,0:T(1,128)} %bitcast.5), custom_call_target="tpu_custom_call" | custom-call | flops 5900000256 | bytes 8000000 | tf_op jit(solution)/shard_map/pallas_call | solution.py:226
  39.2 1.9 %copy.7 = bf16[64,2,16,64]{3,2,1,0:T(8,128)(2,1)} copy(bf16[64,2,16,64]{3,2,1,0:T(8,128)(2,1)} %shard_map.55) | data formatting | bytes 524288

commit v3 on v2

v3 whole, which is shorter than its diff:
```python
import jax
import jax.numpy as jnp
from jax import lax
from jax.experimental import pallas as pl
from jax.experimental.pallas import tpu as pltpu
from jax.sharding import PartitionSpec as P

MESH = pl.DeviceIdType.MESH
F32, BF16 = jnp.float32, jnp.bfloat16
CHAN = 4
SLAB = 64
E2, E1, O0, O1, I1 = range(-2, 3)
PLANE_ONE = {E1: 0, E2: 1, O0: 2, O1: 3, I1: 4}
PLANE_TWO = {E1: 0, O0: 1, O1: 2, I1: 3}
FIRST_ONE, FIRST_TWO = -2, -1
OWN_ONE, OWN_TWO = slice(2, 6), slice(1, 5)


def leaky(value):
    return jnp.where(value >= 0.0, value, 0.3 * value)


def nt(a, b):
    return lax.dot_general(a, b, (((1,), (1,)), ((), ())), preferred_element_type=F32)


def shifted_rows(low, mid, high):
    rows = low.shape[0]
    z = lax.broadcasted_iota(jnp.int32, low.shape, 0) % 64
    up = jnp.where(z == 0, 0.0, pltpu.roll(low, 1, 0))
    down = jnp.where(z == 63, 0.0, pltpu.roll(high, rows - 1, 0))
    return mid + up + down


def shifted_lanes(low, mid, high):
    parts = []
    for first in range(0, low.shape[1], 128):
        cut = slice(first, first + 128)
        z = lax.broadcasted_iota(jnp.int32, (low.shape[0], 128), 1) % 64
        up = jnp.where(z == 0, 0.0, pltpu.roll(low[:, cut], 1, 1))
        down = jnp.where(z == 63, 0.0, pltpu.roll(high[:, cut], 127, 1))
        parts.append(mid[:, cut] + up + down)
    return jnp.concatenate(parts, axis=1)


def accumulate(block, plane_of, first_row, planes, step, filters, channels_first):
    sums = [None] * 3
    for a in range(3):
        for b in range(3):
            pieces = [
                block[plane_of[p + a - 1], y + (b - 1 - first_row)] for p in planes for y in (1 - step, 2 + step)
            ]
            voxels = jnp.concatenate(pieces, axis=0)
            for c in range(3):
                taps = filters[9 * a + 3 * b + c]
                term = nt(taps, voxels) if channels_first else nt(voxels, taps)
                sums[c] = term if sums[c] is None else sums[c] + term
    return sums


def kernel(
    vol, f1, b1, f2, b2, got,
    one, two, w1, w2, bias, mine, local, send_sems, recv_sems, relay,
):
    s, j = lax.axis_index("space"), lax.axis_index("chan")
    flip = s % 2
    sib, ext = s + 1 - 2 * flip, s - 1 + 2 * flip
    has_ext = (ext >= 0) & (ext < lax.axis_size("space"))
    has_up, has_down = j > 0, j < CHAN - 1
    half = lax.axis_size("space") // 2
    seam = (s == half - 1) | (s == half)

    loads = [
        pltpu.make_async_copy(vol.at[flip], one.at[2, OWN_ONE], local.at[0]),
        pltpu.make_async_copy(vol.at[1 - flip], one.at[3, OWN_ONE], local.at[1]),
    ]
    for n, (src, dst) in enumerate(((f1, w1), (f2, w2))):
        for a in range(3):
            first = 9 * (a + flip * (2 - 2 * a))
            loads.append(pltpu.make_async_copy(src.at[pl.ds(first, 9)], dst.at[9 * a : 9 * a + 9], local.at[2 + 3 * n + a]))
    loads.append(pltpu.make_async_copy(b1, bias.at[0], local.at[8]))
    loads.append(pltpu.make_async_copy(b2, bias.at[1], local.at[9]))
    for load in loads[:2]:
        load.start()

    barrier = pltpu.get_barrier_semaphore()
    pl.semaphore_signal(barrier, inc=1, device_id=(sib, j), device_id_type=MESH)
    greeted = ((has_ext, (ext, j)), (has_up, (s, j - 1)), (has_down, (s, j + 1)))
    for there, who in greeted:
        @pl.when(there)
        def _(who=who):
            pl.semaphore_signal(barrier, inc=1, device_id=who, device_id_type=MESH)
    for load in loads[2:]:
        load.start()

    def clear(ref, place):
        ref[place] = jnp.zeros(ref.at[place].shape, BF16)

    for block, outer, above, below in ((one, slice(0, 2), (0, 1), (6, 7)), (two, 0, (0,), (5,))):
        pl.when(~has_ext)(lambda block=block, outer=outer: clear(block, (outer,)))
        for there, places in ((has_up, above), (has_down, below)):
            for place in places:
                pl.when(~there)(lambda block=block, place=place: clear(block, (slice(None), place)))

    used = []

    def remote(src, dst, to, sends, receives):
        n = len(used)
        copy = pltpu.make_async_remote_copy(
            src_ref=src, dst_ref=dst, send_sem=send_sems.at[n], recv_sem=recv_sems.at[n],
            device_id=to, device_id_type=MESH,
        )
        used.append((copy, sends, receives))
        return used[-1]

    def start(*copies):
        for copy, sends, _ in copies:
            copy.start() if sends is True else pl.when(sends)(copy.start)

    def arrived(*copies):
        for copy, _, receives in copies:
            copy.wait_recv() if receives is True else pl.when(receives)(copy.wait_recv)

    sibling, outside, above, below = (sib, j), (ext, j), (s, j - 1), (s, j + 1)
    to_sib = remote(one.at[3, OWN_ONE], one.at[4, OWN_ONE], sibling, True, True)
    to_ext = remote(one.at[2:4, OWN_ONE], one.at[0:2, OWN_ONE], outside, has_ext, has_ext)
    near = (
        remote(one.at[2:4, 2], one.at[2:4, 6], above, has_up, has_down),
        remote(one.at[2:4, 5], one.at[2:4, 1], below, has_down, has_up),
    )
    far = (
        remote(one.at[2:4, 3], one.at[2:4, 7], above, has_up, has_down),
        remote(one.at[2:4, 4], one.at[2:4, 0], below, has_down, has_up),
    )
    near_seam = (
        remote(one.at[0:2, 2], one.at[0:2, 6], above, seam & has_up, seam & has_down),
        remote(one.at[0:2, 5], one.at[0:2, 1], below, seam & has_down, seam & has_up),
    )
    far_seam = (
        remote(one.at[0:2, 3], one.at[0:2, 7], above, seam & has_up, seam & has_down),
        remote(one.at[0:2, 4], one.at[0:2, 0], below, seam & has_down, seam & has_up),
    )

    def corners(r_up, r_down):
        copies = []
        for r, there in ((r_up, has_up), (r_down, has_down)):
            passed = has_ext & ~seam & there
            copies.append(remote(one.at[2:4, r], one.at[0:2, r], outside, passed, passed))
            copies.append(remote(one.at[3, r], one.at[4, r], sibling, there, there))
        return copies

    near_corners, far_corners = corners(1, 6), corners(0, 7)
    inner_two = remote(two.at[2, OWN_TWO], two.at[3, OWN_TWO], sibling, True, True)
    outer_two = [remote(two.at[2, r], two.at[3, r], sibling, there, there) for r, there in ((0, has_up), (5, has_down))]
    own_slab = pl.ds(pl.multiple_of(j * SLAB, SLAB), SLAB)
    turns = []
    for n in range(2):
        turns.append([])
        for step in (2, 1, 3):
            to = (j + step) % CHAN
            turns[n].append(remote(
                mine.at[n, pl.ds(pl.multiple_of(to * SLAB, SLAB), SLAB)], got.at[n, j], (s, to), True, True
            ))

    loads[0].wait()
    loads[1].wait()
    pl.semaphore_wait(barrier, 1 + sum(there.astype(jnp.int32) for there, _ in greeted))
    pl.when(seam)(to_ext[0].start)
    start(*near)
    pl.when(has_ext & ~seam)(to_ext[0].start)
    start(to_sib, *far)

    arrived(*near)
    start(*near_corners)
    for at, tell in ((1, 0), (2, 3)):
        @pl.when(j == at)
        def _(tell=tell):
            pl.semaphore_signal(relay, inc=1, device_id=(s, tell), device_id_type=MESH)
    for load in loads[2:5] + loads[8:]:
        load.wait()
    bias1 = bias[0]

    def hidden(step, carry):
        @pl.when(step == 0)
        def _():
            arrived(to_ext)
            start(*near_seam, *far_seam)
            arrived(to_sib)

        @pl.when(step == 1)
        def _():
            arrived(*far)
            start(*far_corners)
            arrived(*near_corners, *near_seam)

        @pl.when(step == 2)
        def _():
            start(inner_two)
            arrived(*far_corners, *far_seam)

        sums = accumulate(one, PLANE_ONE, FIRST_ONE, (E1, O0, O1), step, w1, False)
        value = leaky(shifted_rows(*sums) + bias1).astype(BF16).reshape(3, 2, 64, 256)
        two[0:3, 2 - step] = value[:, 0]
        two[0:3, 3 + step] = value[:, 1]
        return carry

    lax.fori_loop(0, 3, hidden, 0)
    pl.when(~has_ext)(lambda: clear(two, (0,)))
    for there, r in ((has_up, 0), (has_down, 5)):
        pl.when(~there)(lambda r=r: clear(two, (slice(None), r)))
    start(*outer_two)
    for load in loads[5:8]:
        load.wait()
    bias2 = jnp.transpose(jnp.broadcast_to(bias[1], (8, 256)))[:, :1]
    arrived(inner_two)
    pl.when((j == 0) | (j == CHAN - 1))(lambda: pl.semaphore_wait(relay, 1))

    def features(step, carry):
        @pl.when(step == 1)
        def _():
            arrived(*outer_two)

        sums = accumulate(two, PLANE_TWO, FIRST_TWO, (O0, O1), step, w2, True)
        value = leaky(shifted_lanes(*sums) + bias2).astype(BF16)
        for q in range(2):
            p = q + flip * (1 - 2 * q)
            mine[step, :, pl.ds(pl.multiple_of(128 * p, 128), 128)] = value[:, 128 * q : 128 * q + 128]
        for n in range(2):
            pl.when(step == n)(lambda n=n: start(*turns[n]))
        pltpu.make_async_copy(mine.at[step, own_slab], got.at[step, j], local.at[10 + step]).start()
        return carry

    lax.fori_loop(0, 2, features, 0)
    for n in range(2):
        pltpu.make_async_copy(mine.at[n, own_slab], got.at[n, j], local.at[10 + n]).wait()
        arrived(*turns[n])
    for copy, sends, _ in used:
        copy.wait_send() if sends is True else pl.when(sends)(copy.wait_send)


def regroup(got, out):
    for p in range(2):
        rows = [None] * 16
        for n in range(2):
            for source in range(CHAN):
                pair = got[n, source, :, 128 * p : 128 * p + 128].astype(F32)
                rows[4 * source + 1 - n] = pair[:, :64]
                rows[4 * source + 2 + n] = pair[:, 64:]
        out[:, p] = pltpu.einshape("yoz->oyz", jnp.stack(rows, axis=0)).astype(BF16)


def on_device(volume, first_filter, first_bias, second_filter, second_bias):
    voxels = jnp.transpose(volume, (1, 2, 3, 0))
    hbm = pl.BlockSpec(memory_space=pltpu.HBM)
    dma = pltpu.SemaphoreType.DMA
    got = pl.pallas_call(
        kernel,
        out_shape=jax.ShapeDtypeStruct((2, CHAN, SLAB, 256), BF16),
        in_specs=[hbm] * 5,
        out_specs=hbm,
        scratch_shapes=[
            pltpu.VMEM((5, 8, 64, 256), BF16),
            pltpu.VMEM((4, 6, 64, 256), BF16),
            pltpu.VMEM((27, 256, 256), BF16),
            pltpu.VMEM((27, 256, 256), BF16),
            pltpu.VMEM((2, 1, 256), F32),
            pltpu.VMEM((2, 256, 256), BF16),
            dma((12,)),
            dma((27,)),
            dma((27,)),
            pltpu.SemaphoreType.REGULAR,
        ],
        compiler_params=pltpu.CompilerParams(
            collective_id=0, has_side_effects=True, vmem_limit_bytes=62 * 2**20
        ),
        cost_estimate=pl.CostEstimate(flops=5_900_000_000, bytes_accessed=8_000_000, transcendentals=0),
    )(voxels, first_filter, first_bias.reshape(1, 256), second_filter, second_bias.reshape(1, 256))
    part = SLAB // 2
    return pl.pallas_call(
        regroup,
        out_shape=jax.ShapeDtypeStruct((SLAB, 2, 16, 64), BF16),
        grid=(2,),
        in_specs=[pl.BlockSpec((2, CHAN, part, 256), lambda i: (0, 0, i, 0))],
        out_specs=pl.BlockSpec((part, 2, 16, 64), lambda i: (i, 0, 0, 0)),
        cost_estimate=pl.CostEstimate(flops=0, bytes_accessed=786432, transcendentals=0),
    )(got)


def solution(mesh):
    in_specs = (P(None, "space", "chan", None), P(), P(), P(), P())
    out_specs = P("chan", "space", None, None)
    return jax.shard_map(
        on_device, mesh=mesh, in_specs=in_specs, out_specs=out_specs, check_vma=False
    )
```

time: 41.2 us -> 36.3 us (0.88)
  the two profiles are of different devices: /device:TPU:31 before, /device:TPU:32 now
where the time goes in v3:
time: 36.3 us; the launch traced here: 36.2 us
  Pallas kernels  36.2 us (100%)
    pallas_call x1, Pallas kernels, on_device(): pl.pallas_call(kernel, out_shape=jax.ShapeDtypeStruct((2, CHAN, SLAB, 256...  34.2 us
    pallas_call x1, Pallas kernels, on_device(): pl.pallas_call(regroup, out_shape=jax.ShapeDtypeStruct((SLAB, 2, 16, 64),...  2.02 us

profile of v3, /device:TPU:32, one launch (start us, length us, event | category | flops | bytes accessed | tf_op | source)
XLA Modules:
  0.0 36.2 jit_solution(4215991046715945746)
XLA Ops:
  0.0 34.2 %shard_map.55.got = bf16[2,4,64,256]{3,2,1,0:T(8,128)(2,1)} custom-call(bf16[2,4,64,256]{3,2,1,0:T(8,128)(2,1)} %bitcast.3, bf16[27,256,256]{2,1,0:T(8,128)(2,1)} %f1.1, f32[1,256]{1,0:T(1,128)} %bitcast.4, bf16[27,256,256]{2,1,0:T(8,128)(2,1)} %f2.1, f32[1,256]{1,0:T(1,128)} %bitcast.5), custom_call_target="tpu_custom_call" | custom-call | flops 5900000256 | bytes 8000000 | tf_op jit(solution)/shard_map/pallas_call | solution.py:256
  34.2 2.0 %shard_map.56 = bf16[64,2,16,64]{3,2,1,0:T(8,128)(2,1)} custom-call(bf16[2,4,64,256]{3,2,1,0:T(8,128)(2,1)} %shard_map.55.got), custom_call_target="tpu_custom_call" | custom-call | bytes 786432 | tf_op jit(solution)/shard_map/pallas_call | solution.py:279

commit v4 on v3

--- a/solution.py
+++ b/solution.py
@@ -12,7 +12,6 @@
 E2, E1, O0, O1, I1 = range(-2, 3)
 PLANE_ONE = {E1: 0, E2: 1, O0: 2, O1: 3, I1: 4}
 PLANE_TWO = {E1: 0, O0: 1, O1: 2, I1: 3}
-FIRST_ONE, FIRST_TWO = -2, -1
 OWN_ONE, OWN_TWO = slice(2, 6), slice(1, 5)
 
 
@@ -43,14 +42,11 @@
     return jnp.concatenate(parts, axis=1)
 
 
-def accumulate(block, plane_of, first_row, planes, step, filters, channels_first):
+def accumulate(block, pieces, filters, channels_first):
     sums = [None] * 3
     for a in range(3):
         for b in range(3):
-            pieces = [
-                block[plane_of[p + a - 1], y + (b - 1 - first_row)] for p in planes for y in (1 - step, 2 + step)
-            ]
-            voxels = jnp.concatenate(pieces, axis=0)
+            voxels = jnp.concatenate([block[place] for place in pieces(a, b)], axis=0)
             for c in range(3):
                 taps = filters[9 * a + 3 * b + c]
                 term = nt(taps, voxels) if channels_first else nt(voxels, taps)
@@ -96,11 +92,10 @@
     def clear(ref, place):
         ref[place] = jnp.zeros(ref.at[place].shape, BF16)
 
-    for block, outer, above, below in ((one, slice(0, 2), (0, 1), (6, 7)), (two, 0, (0,), (5,))):
-        pl.when(~has_ext)(lambda block=block, outer=outer: clear(block, (outer,)))
-        for there, places in ((has_up, above), (has_down, below)):
-            for place in places:
-                pl.when(~there)(lambda block=block, place=place: clear(block, (slice(None), place)))
+    pl.when(~has_ext)(lambda: clear(one, (slice(0, 2),)))
+    for there, places in ((has_up, (0, 1)), (has_down, (6, 7))):
+        for place in places:
+            pl.when(~there)(lambda place=place: clear(one, (slice(None), place)))
 
     used = []
 
@@ -142,16 +137,16 @@
     )
 
     def corners(r_up, r_down):
-        copies = []
+        outward, inward = [], []
         for r, there in ((r_up, has_up), (r_down, has_down)):
             passed = has_ext & ~seam & there
-            copies.append(remote(one.at[2:4, r], one.at[0:2, r], outside, passed, passed))
-            copies.append(remote(one.at[3, r], one.at[4, r], sibling, there, there))
-        return copies
-
-    near_corners, far_corners = corners(1, 6), corners(0, 7)
-    inner_two = remote(two.at[2, OWN_TWO], two.at[3, OWN_TWO], sibling, True, True)
-    outer_two = [remote(two.at[2, r], two.at[3, r], sibling, there, there) for r, there in ((0, has_up), (5, has_down))]
+            outward.append(remote(one.at[2:4, r], one.at[0:2, r], outside, passed, passed))
+            inward.append(remote(one.at[3, r], one.at[4, r], sibling, there, there))
+        return outward, inward
+
+    near_outward, near_inward = corners(1, 6)
+    far_outward, far_inward = corners(0, 7)
+    plane_two = remote(two.at[2], two.at[3], sibling, True, True)
     own_slab = pl.ds(pl.multiple_of(j * SLAB, SLAB), SLAB)
     turns = []
     for n in range(2):
@@ -168,10 +163,15 @@
     pl.when(seam)(to_ext[0].start)
     start(*near)
     pl.when(has_ext & ~seam)(to_ext[0].start)
-    start(to_sib, *far)
+    busy = ((s + 2) % half < 4) & ~seam
+    start(to_sib)
+    for copy, sends, _ in far:
+        pl.when(sends & ~busy)(copy.start)
 
     arrived(*near)
-    start(*near_corners)
+    start(*near_outward, *near_inward)
+    for copy, sends, _ in far:
+        pl.when(sends & busy)(copy.start)
     for at, tell in ((1, 0), (2, 3)):
         @pl.when(j == at)
         def _(tell=tell):
@@ -179,58 +179,80 @@
     for load in loads[2:5] + loads[8:]:
         load.wait()
     bias1 = bias[0]
-
-    def hidden(step, carry):
-        @pl.when(step == 0)
-        def _():
-            arrived(to_ext)
-            start(*near_seam, *far_seam)
-            arrived(to_sib)
-
-        @pl.when(step == 1)
-        def _():
-            arrived(*far)
-            start(*far_corners)
-            arrived(*near_corners, *near_seam)
-
-        @pl.when(step == 2)
-        def _():
-            start(inner_two)
-            arrived(*far_corners, *far_seam)
-
-        sums = accumulate(one, PLANE_ONE, FIRST_ONE, (E1, O0, O1), step, w1, False)
-        value = leaky(shifted_rows(*sums) + bias1).astype(BF16).reshape(3, 2, 64, 256)
-        two[0:3, 2 - step] = value[:, 0]
-        two[0:3, 3 + step] = value[:, 1]
-        return carry
-
-    lax.fori_loop(0, 3, hidden, 0)
-    pl.when(~has_ext)(lambda: clear(two, (0,)))
-    for there, r in ((has_up, 0), (has_down, 5)):
-        pl.when(~there)(lambda r=r: clear(two, (slice(None), r)))
-    start(*outer_two)
+    arrived(to_ext)
+    start(*near_seam, *far_seam)
+    arrived(to_sib)
+
+    def hidden(pieces):
+        return leaky(shifted_rows(*accumulate(one, pieces, w1, False)) + bias1).astype(BF16).reshape(-1, 64, 256)
+
+    value = hidden(lambda a, b: [(PLANE_ONE[p + a - 1], y + b + 1) for p in (E1, O0, O1) for y in (1, 2)])
+    two[0:3, 2:4] = value.reshape(3, 2, 64, 256)
     for load in loads[5:8]:
         load.wait()
     bias2 = jnp.transpose(jnp.broadcast_to(bias[1], (8, 256)))[:, :1]
-    arrived(inner_two)
-    pl.when((j == 0) | (j == CHAN - 1))(lambda: pl.semaphore_wait(relay, 1))
-
-    def features(step, carry):
+
+    def clear_rows(planes):
+        for there, r in ((has_up, 0), (has_down, 5)):
+            pl.when(~there)(lambda r=r: clear(two, (planes, r)))
+
+    def block(step, carry):
+        @pl.when(step == 0)
+        def _():
+            arrived(*far)
+            start(*far_outward, *far_inward)
+            arrived(*near_inward, *far_inward)
+
         @pl.when(step == 1)
         def _():
-            arrived(*outer_two)
-
-        sums = accumulate(two, PLANE_TWO, FIRST_TWO, (O0, O1), step, w2, True)
-        value = leaky(shifted_lanes(*sums) + bias2).astype(BF16)
+            arrived(*near_outward, *near_seam)
+
+        @pl.when(step == 2)
+        def _():
+            arrived(*far_outward, *far_seam)
+
+        at_o1 = (2 - step) // 2
+        rows = (-(step // 2), 3 + step // 2, step % 2 - 1, 4 - step % 2)
+
+        def place(a, i):
+            other = PLANE_ONE[(O0, E1)[i // 2] + a - 1]
+            return other + at_o1 * (PLANE_ONE[O1 + a - 1] - other)
+
+        value = hidden(lambda a, b: [(place(a, i), rows[i] + b + 1) for i in range(4)])
+        for i in range(4):
+            other = PLANE_TWO[(O0, E1)[i // 2]]
+            two[other + at_o1 * (PLANE_TWO[O1] - other), rows[i] + 1] = value[i]
+
+        @pl.when(step == 0)
+        def _():
+            clear_rows(2)
+            start(plane_two)
+
+        @pl.when(step == 1)
+        def _():
+            pl.when(~has_ext)(lambda: clear(two, (0,)))
+            arrived(plane_two)
+            pl.when((j == 0) | (j == CHAN - 1))(lambda: pl.semaphore_wait(relay, 1))
+
+        @pl.when(step == 2)
+        def _():
+            pl.when(~has_ext)(lambda: clear(two, (0,)))
+            clear_rows(slice(0, 2))
+
+        pl.when(step > 0)(lambda: features(step - 1))
+        return carry
+
+    def features(n):
+        pieces = lambda a, b: [(PLANE_TWO[p + a - 1], y + b) for p in (O0, O1) for y in (1 - n, 2 + n)]
+        value = leaky(shifted_lanes(*accumulate(two, pieces, w2, True)) + bias2).astype(BF16)
         for q in range(2):
             p = q + flip * (1 - 2 * q)
-            mine[step, :, pl.ds(pl.multiple_of(128 * p, 128), 128)] = value[:, 128 * q : 128 * q + 128]
-        for n in range(2):
-            pl.when(step == n)(lambda n=n: start(*turns[n]))
-        pltpu.make_async_copy(mine.at[step, own_slab], got.at[step, j], local.at[10 + step]).start()
-        return carry
-
-    lax.fori_loop(0, 2, features, 0)
+            mine[n, :, pl.ds(pl.multiple_of(128 * p, 128), 128)] = value[:, 128 * q : 128 * q + 128]
+        for k in range(2):
+            pl.when(n == k)(lambda k=k: start(*turns[k]))
+        pltpu.make_async_copy(mine.at[n, own_slab], got.at[n, j], local.at[10 + n]).start()
+
+    lax.fori_loop(0, 3, block, 0)
     for n in range(2):
         pltpu.make_async_copy(mine.at[n, own_slab], got.at[n, j], local.at[10 + n]).wait()
         arrived(*turns[n])
@@ -266,8 +288,8 @@
             pltpu.VMEM((2, 1, 256), F32),
             pltpu.VMEM((2, 256, 256), BF16),
             dma((12,)),
-            dma((27,)),
-            dma((27,)),
+            dma((28,)),
+            dma((28,)),
             pltpu.SemaphoreType.REGULAR,
         ],
         compiler_params=pltpu.CompilerParams(

time: 36.3 us -> 34.2 us (0.942)
  Pallas kernels: 36.2 us -> 34.1 us
    pallas_call x1, Pallas kernels: 34.2 us -> 32.1 us  [on_device(): pl.pallas_call(kernel, out_shape=jax.ShapeDtypeStruct((2, CHAN, SLAB, 256...]
where the time goes in v4:
time: 34.2 us
  Pallas kernels  34.1 us (100%)
    pallas_call x1, Pallas kernels, on_device(): pl.pallas_call(kernel, out_shape=jax.ShapeDtypeStruct((2, CHAN, SLAB, 256...  32.1 us
    pallas_call x1, Pallas kernels, on_device(): pl.pallas_call(regroup, out_shape=jax.ShapeDtypeStruct((SLAB, 2, 16, 64),...  2.02 us

profile of v4, /device:TPU:32, one launch (start us, length us, event | category | flops | bytes accessed | tf_op | source)
XLA Modules:
  0.0 34.2 jit_solution(16256262603782990878)
XLA Ops:
  0.0 32.1 %shard_map.55.got = bf16[2,4,64,256]{3,2,1,0:T(8,128)(2,1)} custom-call(bf16[2,4,64,256]{3,2,1,0:T(8,128)(2,1)} %bitcast.3, bf16[27,256,256]{2,1,0:T(8,128)(2,1)} %f1.1, f32[1,256]{1,0:T(1,128)} %bitcast.4, bf16[27,256,256]{2,1,0:T(8,128)(2,1)} %f2.1, f32[1,256]{1,0:T(1,128)} %bitcast.5), custom_call_target="tpu_custom_call" | custom-call | flops 5900000256 | bytes 8000000 | tf_op jit(solution)/shard_map/pallas_call | solution.py:278
  32.1 2.0 %shard_map.56 = bf16[64,2,16,64]{3,2,1,0:T(8,128)(2,1)} custom-call(bf16[2,4,64,256]{3,2,1,0:T(8,128)(2,1)} %shard_map.55.got), custom_call_target="tpu_custom_call" | custom-call | bytes 786432 | tf_op jit(solution)/shard_map/pallas_call | solution.py:301

commit v5 on v4

--- a/solution.py
+++ b/solution.py
@@ -12,7 +12,7 @@
 E2, E1, O0, O1, I1 = range(-2, 3)
 PLANE_ONE = {E1: 0, E2: 1, O0: 2, O1: 3, I1: 4}
 PLANE_TWO = {E1: 0, O0: 1, O1: 2, I1: 3}
-OWN_ONE, OWN_TWO = slice(2, 6), slice(1, 5)
+OWN_ONE = slice(2, 6)
 
 
 def leaky(value):
@@ -127,25 +127,21 @@
         remote(one.at[2:4, 3], one.at[2:4, 7], above, has_up, has_down),
         remote(one.at[2:4, 4], one.at[2:4, 0], below, has_down, has_up),
     )
-    near_seam = (
-        remote(one.at[0:2, 2], one.at[0:2, 6], above, seam & has_up, seam & has_down),
-        remote(one.at[0:2, 5], one.at[0:2, 1], below, seam & has_down, seam & has_up),
-    )
     far_seam = (
         remote(one.at[0:2, 3], one.at[0:2, 7], above, seam & has_up, seam & has_down),
         remote(one.at[0:2, 4], one.at[0:2, 0], below, seam & has_down, seam & has_up),
     )
 
-    def corners(r_up, r_down):
+    def corners(r_up, r_down, outer):
         outward, inward = [], []
         for r, there in ((r_up, has_up), (r_down, has_down)):
-            passed = has_ext & ~seam & there
+            passed = outer & there
             outward.append(remote(one.at[2:4, r], one.at[0:2, r], outside, passed, passed))
             inward.append(remote(one.at[3, r], one.at[4, r], sibling, there, there))
         return outward, inward
 
-    near_outward, near_inward = corners(1, 6)
-    far_outward, far_inward = corners(0, 7)
+    near_outward, near_inward = corners(1, 6, has_ext)
+    far_outward, far_inward = corners(0, 7, has_ext & ~seam)
     plane_two = remote(two.at[2], two.at[3], sibling, True, True)
     own_slab = pl.ds(pl.multiple_of(j * SLAB, SLAB), SLAB)
     turns = []
@@ -180,7 +176,7 @@
         load.wait()
     bias1 = bias[0]
     arrived(to_ext)
-    start(*near_seam, *far_seam)
+    start(*far_seam)
     arrived(to_sib)
 
     def hidden(pieces):
@@ -205,7 +201,7 @@
 
         @pl.when(step == 1)
         def _():
-            arrived(*near_outward, *near_seam)
+            arrived(*near_outward)
 
         @pl.when(step == 2)
         def _():
@@ -288,8 +284,8 @@
             pltpu.VMEM((2, 1, 256), F32),
             pltpu.VMEM((2, 256, 256), BF16),
             dma((12,)),
-            dma((28,)),
-            dma((28,)),
+            dma((26,)),
+            dma((26,)),
             pltpu.SemaphoreType.REGULAR,
         ],
         compiler_params=pltpu.CompilerParams(

time: 34.2 us -> 33.9 us (level)
    pallas_call x1, Pallas kernels: 32.1 us -> 31.8 us  [on_device(): pl.pallas_call(kernel, out_shape=jax.ShapeDtypeStruct((2, CHAN, SLAB, 256...]
where the time goes in v5:
time: 33.9 us; the launch traced here: 33.8 us
  Pallas kernels  33.8 us (100%)
    pallas_call x1, Pallas kernels, on_device(): pl.pallas_call(kernel, out_shape=jax.ShapeDtypeStruct((2, CHAN, SLAB, 256...  31.8 us
    pallas_call x1, Pallas kernels, on_device(): pl.pallas_call(regroup, out_shape=jax.ShapeDtypeStruct((SLAB, 2, 16, 64),...  2.02 us

profile of v5, /device:TPU:32, one launch (start us, length us, event | category | flops | bytes accessed | tf_op | source)
XLA Modules:
  0.0 33.8 jit_solution(4302242612193111794)
XLA Ops:
  0.0 31.8 %shard_map.55.got = bf16[2,4,64,256]{3,2,1,0:T(8,128)(2,1)} custom-call(bf16[2,4,64,256]{3,2,1,0:T(8,128)(2,1)} %bitcast.3, bf16[27,256,256]{2,1,0:T(8,128)(2,1)} %f1.1, f32[1,256]{1,0:T(1,128)} %bitcast.4, bf16[27,256,256]{2,1,0:T(8,128)(2,1)} %f2.1, f32[1,256]{1,0:T(1,128)} %bitcast.5), custom_call_target="tpu_custom_call" | custom-call | flops 5900000256 | bytes 8000000 | tf_op jit(solution)/shard_map/pallas_call | solution.py:274
  31.8 2.0 %shard_map.56 = bf16[64,2,16,64]{3,2,1,0:T(8,128)(2,1)} custom-call(bf16[2,4,64,256]{3,2,1,0:T(8,128)(2,1)} %shard_map.55.got), custom_call_target="tpu_custom_call" | custom-call | bytes 786432 | tf_op jit(solution)/shard_map/pallas_call | solution.py:297

commit v6 on v5

--- a/solution.py
+++ b/solution.py
@@ -256,26 +256,33 @@
         copy.wait_send() if sends is True else pl.when(sends)(copy.wait_send)
 
 
-def regroup(got, out):
-    for p in range(2):
-        rows = [None] * 16
-        for n in range(2):
-            for source in range(CHAN):
-                pair = got[n, source, :, 128 * p : 128 * p + 128].astype(F32)
-                rows[4 * source + 1 - n] = pair[:, :64]
-                rows[4 * source + 2 + n] = pair[:, 64:]
-        out[:, p] = pltpu.einshape("yoz->oyz", jnp.stack(rows, axis=0)).astype(BF16)
+def regroup(got, out, built, sems):
+    part, copies = SLAB // 2, []
+    for k in range(2):
+        channels = slice(part * k, part * k + part)
+        for p in range(2):
+            rows = [None] * 16
+            for n in range(2):
+                for source in range(CHAN):
+                    pair = got[n, source, channels, 128 * p : 128 * p + 128].astype(F32)
+                    rows[4 * source + 1 - n] = pair[:, :64]
+                    rows[4 * source + 2 + n] = pair[:, 64:]
+            built[channels, p] = pltpu.einshape("yoz->oyz", jnp.stack(rows, axis=0)).astype(BF16)
+        copies.append(pltpu.make_async_copy(built.at[channels], out.at[channels], sems.at[k]))
+        copies[k].start()
+    for copy in copies:
+        copy.wait()
 
 
 def on_device(volume, first_filter, first_bias, second_filter, second_bias):
     voxels = jnp.transpose(volume, (1, 2, 3, 0))
-    hbm = pl.BlockSpec(memory_space=pltpu.HBM)
+    hbm, vmem = pl.BlockSpec(memory_space=pltpu.HBM), pl.BlockSpec(memory_space=pltpu.VMEM)
     dma = pltpu.SemaphoreType.DMA
     got = pl.pallas_call(
         kernel,
-        out_shape=jax.ShapeDtypeStruct((2, CHAN, SLAB, 256), BF16),
+        out_shape=pltpu.VMEM((2, CHAN, SLAB, 256), BF16),
         in_specs=[hbm] * 5,
-        out_specs=hbm,
+        out_specs=vmem,
         scratch_shapes=[
             pltpu.VMEM((5, 8, 64, 256), BF16),
             pltpu.VMEM((4, 6, 64, 256), BF16),
@@ -293,13 +300,13 @@
         ),
         cost_estimate=pl.CostEstimate(flops=5_900_000_000, bytes_accessed=8_000_000, transcendentals=0),
     )(voxels, first_filter, first_bias.reshape(1, 256), second_filter, second_bias.reshape(1, 256))
-    part = SLAB // 2
     return pl.pallas_call(
         regroup,
         out_shape=jax.ShapeDtypeStruct((SLAB, 2, 16, 64), BF16),
-        grid=(2,),
-        in_specs=[pl.BlockSpec((2, CHAN, part, 256), lambda i: (0, 0, i, 0))],
-        out_specs=pl.BlockSpec((part, 2, 16, 64), lambda i: (i, 0, 0, 0)),
+        in_specs=[vmem],
+        out_specs=hbm,
+        scratch_shapes=[pltpu.VMEM((SLAB, 2, 16, 64), BF16), dma((2,))],
+        compiler_params=pltpu.CompilerParams(vmem_limit_bytes=8 * 2**20),
         cost_estimate=pl.CostEstimate(flops=0, bytes_accessed=786432, transcendentals=0),
     )(got)
 

time: 33.9 us -> 32.8 us (0.968)
  Pallas kernels: 33.8 us -> 32.7 us
    pallas_call x1, Pallas kernels: 2.02 us -> 1.02 us  [on_device(): pl.pallas_call(regroup, out_shape=jax.ShapeDtypeStruct((SLAB, 2, 16, 64),...]
where the time goes in v6:
time: 32.8 us; the launch traced here: 32.7 us
  Pallas kernels  32.7 us (100%)
    pallas_call x1, Pallas kernels, on_device(): pl.pallas_call(kernel, out_shape=pltpu.VMEM((2, CHAN, SLAB, 256), BF16),...  31.7 us
    pallas_call x1, Pallas kernels, on_device(): pl.pallas_call(regroup, out_shape=jax.ShapeDtypeStruct((SLAB, 2, 16, 64),...  1.02 us

profile of v6, /device:TPU:32, one launch (start us, length us, event | category | flops | bytes accessed | tf_op | source)
XLA Modules:
  0.0 32.7 jit_solution(17136614124359924386)
XLA Ops:
  0.0 31.7 %shard_map.55.got = bf16[2,4,64,256]{3,2,1,0:T(8,128)(2,1)S(1)} custom-call(bf16[2,4,64,256]{3,2,1,0:T(8,128)(2,1)} %bitcast.3, bf16[27,256,256]{2,1,0:T(8,128)(2,1)} %f1.1, f32[1,256]{1,0:T(1,128)} %bitcast.4, bf16[27,256,256]{2,1,0:T(8,128)(2,1)} %f2.1, f32[1,256]{1,0:T(1,128)} %bitcast.5), custom_call_target="tpu_custom_call" | custom-call | flops 5900000256 | bytes 8000000 | tf_op jit(solution)/shard_map/pallas_call | solution.py:281
  31.7 1.0 %shard_map.56 = bf16[64,2,16,64]{3,2,1,0:T(8,128)(2,1)} custom-call(bf16[2,4,64,256]{3,2,1,0:T(8,128)(2,1)S(1)} %shard_map.55.got), custom_call_target="tpu_custom_call" | custom-call | bytes 786432 | tf_op jit(solution)/shard_map/pallas_call | solution.py:303

commit v7 on v6

--- a/solution.py
+++ b/solution.py
@@ -268,8 +268,8 @@
                     rows[4 * source + 1 - n] = pair[:, :64]
                     rows[4 * source + 2 + n] = pair[:, 64:]
             built[channels, p] = pltpu.einshape("yoz->oyz", jnp.stack(rows, axis=0)).astype(BF16)
-        copies.append(pltpu.make_async_copy(built.at[channels], out.at[channels], sems.at[k]))
-        copies[k].start()
+            copies.append(pltpu.make_async_copy(built.at[channels, p], out.at[channels, p], sems.at[2 * k + p]))
+            copies[-1].start()
     for copy in copies:
         copy.wait()
 
@@ -305,7 +305,7 @@
         out_shape=jax.ShapeDtypeStruct((SLAB, 2, 16, 64), BF16),
         in_specs=[vmem],
         out_specs=hbm,
-        scratch_shapes=[pltpu.VMEM((SLAB, 2, 16, 64), BF16), dma((2,))],
+        scratch_shapes=[pltpu.VMEM((SLAB, 2, 16, 64), BF16), dma((4,))],
         compiler_params=pltpu.CompilerParams(vmem_limit_bytes=8 * 2**20),
         cost_estimate=pl.CostEstimate(flops=0, bytes_accessed=786432, transcendentals=0),
     )(got)

time: 32.8 us -> 32.8 us (level)
  no operation moved by 1% of the time
where the time goes in v7:
time: 32.8 us; the launch traced here: 32.7 us
  Pallas kernels  32.7 us (100%)
    pallas_call x1, Pallas kernels, on_device(): pl.pallas_call(kernel, out_shape=pltpu.VMEM((2, CHAN, SLAB, 256), BF16),...  31.7 us
    pallas_call x1, Pallas kernels, on_device(): pl.pallas_call(regroup, out_shape=jax.ShapeDtypeStruct((SLAB, 2, 16, 64),...  0.99 us

profile of v7, /device:TPU:32, one launch (start us, length us, event | category | flops | bytes accessed | tf_op | source)
XLA Modules:
  0.0 32.7 jit_solution(6252183237077886542)
XLA Ops:
  0.0 31.7 %shard_map.55.got = bf16[2,4,64,256]{3,2,1,0:T(8,128)(2,1)S(1)} custom-call(bf16[2,4,64,256]{3,2,1,0:T(8,128)(2,1)} %bitcast.3, bf16[27,256,256]{2,1,0:T(8,128)(2,1)} %f1.1, f32[1,256]{1,0:T(1,128)} %bitcast.4, bf16[27,256,256]{2,1,0:T(8,128)(2,1)} %f2.1, f32[1,256]{1,0:T(1,128)} %bitcast.5), custom_call_target="tpu_custom_call" | custom-call | flops 5900000256 | bytes 8000000 | tf_op jit(solution)/shard_map/pallas_call | solution.py:281
  31.7 1.0 %shard_map.56 = bf16[64,2,16,64]{3,2,1,0:T(8,128)(2,1)} custom-call(bf16[2,4,64,256]{3,2,1,0:T(8,128)(2,1)S(1)} %shard_map.55.got), custom_call_target="tpu_custom_call" | custom-call | bytes 786432 | tf_op jit(solution)/shard_map/pallas_call | solution.py:303
